TPU v7x, 32 devices: a whole 2x2x4 slice. The times are simulated.
32 devices in a mesh: gx: 16 (over z, y, core), gz: 2 (over x).
Axes of the slice: x: 2, y: 2, z: 4, core: 2. Of those that a mesh axis runs over, the one named last changes fastest.
Arguments:
- strain_inc: float32 [6, 32, 256, 256], P(None, 'gx', None, 'gz'), may hold values from -2.5 to 2.5
- stress_old: float32 [6, 32, 256, 256], P(None, 'gx', None, 'gz'), may hold values from -6 to 6
- material_id: int32 [32, 256, 256], P('gx', None, 'gz'), may hold values from 0 to 7
- cohesion: float32 [8], replicated, may hold values from 1 to 4
- friction: float32 [8], replicated, may hold values from 0.05 to 0.3
- pressure: float32 [32, 256, 256], P('gx', 'gz'), may hold values from -6 to 6
- storage: float32 [32, 256, 256], P('gx', 'gz'), may hold values from 0.5 to 4
- perm_class: int32 [32, 256, 256], P('gx', 'gz'), may hold values from 0 to 15
- perm_table: float32 [16], replicated, may hold values from 0.5 to 8
Outputs:
- pressure_next: float32 [32, 256, 256], P('gx', 'gz')
- stress_next: float32 [6, 32, 256, 256], P(None, 'gx', None, 'gz')
- node_force: float32 [3, 32, 256, 256], P(None, 'gx', None, 'gz')
All inputs are finite; a program needn't handle non-finite values.
Results may differ from a plain program's by a relative error of at most 0.00002.
Values sent between devices are 32-bit elements; how exact they have to be, the bound alone decides.
A program may use at most 64 MiB of HBM per device.

v0:
```python
import jax
import jax.numpy as jnp
from jax import lax
from jax.sharding import PartitionSpec as P

BIOT = 0.8
SHEAR = 1.0
BULK = 1.5
FLOOR = 0.25
TINY = 1e-30


def extended(array, sides, width):
    for axis, dim in sides:
        count, length = (lax.axis_size(axis), array.shape[dim])
        up = [(i, (i + 1) % count) for i in range(count - 1)]
        down = [(j, i) for i, j in up]
        last = lax.slice_in_dim(array, length - width, length, axis=dim)
        leading = lax.slice_in_dim(array, 0, width, axis=dim)
        before = lax.ppermute(last, axis, up)
        after = lax.ppermute(leading, axis, down)
        array = jnp.concatenate([before, array, after], axis=dim)
    return array


def passed_along(block, axis, distance):
    devices = range(lax.axis_size(axis))
    route = [(i - distance, i) for i in devices if i - distance in devices]
    return lax.ppermute(block, axis, route)


def lookup(ids, table):
    result = jnp.zeros(ids.shape, jnp.float32)
    for entry in range(table.shape[0]):
        result = result + jnp.where(ids == entry, table[entry], jnp.zeros((), jnp.float32))
    return result


def neighbours():
    inner = slice(1, -1)
    return [
        (slice(2, None), inner, inner),
        (slice(0, -2), inner, inner),
        (inner, slice(2, None), inner),
        (inner, slice(0, -2), inner),
        (inner, inner, slice(2, None)),
        (inner, inner, slice(0, -2)),
    ]


def relax_padded(pressure_pad, cond_pad, storage, source):
    conduct = cond_pad[1:-1, 1:-1, 1:-1]
    numerator = source
    denominator = storage
    for offset in neighbours():
        cond_near = cond_pad[offset]
        transmit = 2.0 * conduct * cond_near / jnp.maximum(conduct + cond_near, TINY)
        numerator = numerator + transmit * pressure_pad[offset]
        denominator = denominator + transmit
    denominator = jnp.where(denominator > 0.0, denominator, jnp.ones((), jnp.float32))
    return numerator / denominator


def plastic(strain_inc, stress_old, material_id, cohesion, friction):
    normal_mask = jnp.array([1.0, 1.0, 1.0, 0.0, 0.0, 0.0], jnp.float32).reshape(6, 1, 1, 1)
    volume = strain_inc[0] + strain_inc[1] + strain_inc[2]
    trial_stress = (
        stress_old
        + 2.0 * SHEAR * (strain_inc - normal_mask * (volume / 3.0))
        + BULK * volume * normal_mask
    )
    first_invariant = trial_stress[0] + trial_stress[1] + trial_stress[2]
    deviator = trial_stress - normal_mask * (first_invariant / 3.0)
    second_invariant = 0.5 * (
        deviator[0] * deviator[0] + deviator[1] * deviator[1] + deviator[2] * deviator[2]
    )
    second_invariant = (
        second_invariant
        + deviator[3] * deviator[3]
        + deviator[4] * deviator[4]
        + deviator[5] * deviator[5]
    )
    equiv_shear = jnp.sqrt(second_invariant)
    strength = lookup(material_id, cohesion)
    slope = lookup(material_id, friction)
    yield_value = equiv_shear + slope * first_invariant - strength
    multiplier = jnp.maximum(yield_value, 0.0) / (SHEAR + 9.0 * BULK * slope * slope)
    shrink_factor = jnp.maximum(1.0 - SHEAR * multiplier / jnp.maximum(equiv_shear, FLOOR), 0.0)
    new_invariant = first_invariant - 9.0 * BULK * slope * multiplier
    return deviator * shrink_factor + normal_mask * (new_invariant / 3.0)


def corner_terms(stress_next, pressure_block):
    normal_mask = jnp.array([1.0, 1.0, 1.0, 0.0, 0.0, 0.0], jnp.float32).reshape(6, 1, 1, 1)
    total = stress_next - BIOT * pressure_block * normal_mask
    col_x = jnp.stack([total[0], total[3], total[5]])
    col_y = jnp.stack([total[3], total[1], total[4]])
    col_z = jnp.stack([total[5], total[4], total[2]])
    return (col_x, col_y, col_z)


def place_corner(term, along_x, along_y):
    placed = jnp.pad(term, ((0, 0), (along_x, 1 - along_x), (0, 0), (0, 0)))
    if along_y == 1:
        placed = jnp.pad(placed, ((0, 0), (0, 0), (1, 0), (0, 0)))[:, :, :-1]
    return placed


def node_parts(col_x, col_y, col_z):
    lower = None
    upper = None
    for corner in range(8):
        along_x = corner & 1
        along_y = corner >> 1 & 1
        along_z = corner >> 2
        term = 0.25 * (
            (2 * along_x - 1) * col_x + (2 * along_y - 1) * col_y + (2 * along_z - 1) * col_z
        )
        placed = place_corner(term, along_x, along_y)
        if along_z == 0:
            lower = placed if lower is None else lower + placed
        else:
            upper = placed if upper is None else upper + placed
    node_main = lower + jnp.pad(upper[..., :-1], ((0, 0), (0, 0), (0, 0), (1, 0)))
    node_rim = upper[..., -1]
    return (node_main, node_rim)


def on_device(
    strain_inc,
    stress_old,
    material_id,
    cohesion,
    friction,
    pressure,
    storage,
    perm_class,
    perm_table,
):
    strain_rate = strain_inc[0] + strain_inc[1] + strain_inc[2]
    rate_column = lax.all_to_all(strain_rate, "gz", split_axis=1, concat_axis=2, tiled=True)
    stress_next = plastic(strain_inc, stress_old, material_id, cohesion, friction)
    conduct = lookup(perm_class, perm_table)
    source = storage * pressure - BIOT * rate_column
    pressure_pair = extended(jnp.stack([pressure, conduct]), (("gx", 1), ("gz", 2)), 1)
    pressure_pair = jnp.pad(pressure_pair, ((0, 0), (0, 0), (0, 0), (1, 1)))
    first_sweep = relax_padded(pressure_pair[0], pressure_pair[1], storage, source)
    bordered = extended(first_sweep, (("gx", 0), ("gz", 1)), 1)
    bordered = jnp.pad(bordered, ((0, 0), (0, 0), (1, 1)))
    pressure_next = relax_padded(bordered, pressure_pair[1], storage, source)
    pressure_block = lax.all_to_all(pressure_next, "gz", split_axis=2, concat_axis=1, tiled=True)
    col_x, col_y, col_z = corner_terms(stress_next, pressure_block)
    node_main, node_rim = node_parts(col_x, col_y, col_z)
    from_below = passed_along(node_rim, "gz", 1)
    node_main = node_main.at[:, :, :, 0].add(from_below)
    slab_plane = passed_along(node_main[:, -1], "gx", 1)
    node_main = node_main.at[:, 0].add(slab_plane)
    node_force = node_main[:, :-1]
    return (pressure_next, stress_next, node_force)


def solution(mesh):
    in_specs = (
        P(None, "gx", None, "gz"),
        P(None, "gx", None, "gz"),
        P("gx", None, "gz"),
        P(),
        P(),
        P("gx", "gz", None),
        P("gx", "gz", None),
        P("gx", "gz", None),
        P(),
    )
    out_specs = (P("gx", "gz", None), P(None, "gx", None, "gz"), P(None, "gx", None, "gz"))
    return jax.shard_map(
        on_device, mesh=mesh, in_specs=in_specs, out_specs=out_specs, check_vma=False
    )
```

profile of v0, /device:TPU:10, one launch (start us, length us, event | category | flops | bytes accessed | tf_op | source)
XLA Modules:
  0.0 118.8 jit_solution(4340846625910367335)
XLA Ops:
  0.6 1.9 %fusion.46 = (f32[1]{0:T(128)}, f32[1]{0:T(128)}, f32[1]{0:T(128)}, f32[1]{0:T(128)}, f32[1]{0:T(128)}, /*index=5*/f32[1]{0:T(128)}, f32[1]{0:T(128)}, f32[1]{0:...) fusion(f32[16]{0:T(128)} %param.23), kind=kLoop, calls=%fused_computation.149 | loop fusion | bytes 128 | tf_op jit(solution)/shard_map/slice | solution.py:35
  2.6 12.0 %add_bitcast_fusion = f32[1,2,128,256]{3,2,1,0:T(8,128)} fusion(s32[2,128,256]{2,1,0:T(8,128)} %param.22, f32[]{:T(128)} %bitcast.19, f32[]{:T(128)} %bitcast.18, f32[]{:T(128)} %bitcast.17, f32[]{:T(128)} %bitcast.16, f32[]{:T(128)} %bitcast.15, f32[]{:T(128)} %bitcast.14, f32[]{:T(128)} %bitcast.13, f32[]{:T(128)} %bitcast.12, f32[]{:T(128)} %bitcast.11, ...), kind=kLoop, calls=%fused_computation.125 | loop fusion | flops 3080192 | bytes 524352 | tf_op jit(solution)/shard_map/stack | solution.py:145
  14.6 1.9 %fusion.11 = (f32[2,1,128,256]{3,2,1,0:T(8,128)}, f32[2,1,128,256]{3,2,1,0:T(8,128)}) fusion(f32[1,2,128,256]{3,2,1,0:T(8,128)} %bitcast.79, f32[1,2,128,256]{3,2,1,0:T(8,128)} %add_bitcast_fusion), kind=kLoop, calls=%fused_computation.57 | loop fusion | flops 131072 | bytes 1048576 | tf_op jit(solution)/shard_map/stack | solution.py:145
  16.5 2.0 %collective-permute-start = (f32[2,1,128,256]{3,2,1,0:T(8,128)}, f32[2,1,128,256]{3,2,1,0:T(8,128)}, u32[]{:S(2)}, u32[]{:S(2)}) collective-permute-start(f32[2,1,128,256]{3,2,1,0:T(8,128)} %get-tuple-element.84), channel_id=1, source_target_pairs={{0,2},{2,4},{4,6},{6,8},{8,10},{10,12},{12,14},{14,16},{16,18},{18... | collective-permute-start | bytes 786440 | tf_op jit(solution)/shard_map/ppermute | solution.py:20
  18.6 4.5 %collective-permute-start.1 = (f32[2,1,128,256]{3,2,1,0:T(8,128)}, f32[2,1,128,256]{3,2,1,0:T(8,128)}, u32[]{:S(2)}, u32[]{:S(2)}) collective-permute-start(f32[2,1,128,256]{3,2,1,0:T(8,128)} %get-tuple-element.85), channel_id=1, source_target_pairs={{2,0},{4,2},{6,4},{8,6},{10,8},{12,10},{14,12},{16,14},{18,16},{20... | collective-permute-start | bytes 786440 | tf_op jit(solution)/shard_map/ppermute | solution.py:21
  23.2 0.9 copy.250
  24.1 4.6 %all-to-all-start = ((f32[2,256,128]{2,0,1:T(2,128)}), f32[2,256,128]{2,0,1:T(2,128)}, u32[]{:S(2)}, u32[]{:S(2)}) async-start(f32[2,256,128]{2,0,1:T(2,128)} %copy.250), calls=%async_computation | async-start | bytes 524288 | tf_op jit(solution)/shard_map/all_to_all | solution.py:141
  28.8 1.8 %multiply_add_fusion.1 = f32[6,2,256,128]{3,2,1,0:T(8,128)S(1)} fusion(f32[6,2,256,128]{3,2,1,0:T(8,128)} %param.16, f32[6,2,256,128]{3,2,1,0:T(8,128)S(1)} %copy-done.1, f32[2,256,128]{2,1,0:T(8,128)S(1)} %multiply_bitcast_fusion.1, f32[2,256,128]{2,1,0:T(8,128)S(1)} %get-tuple-element.62, f32[6]{0:T(128)S(1)} %copy-done.18), kind=kLoop, calls=%fused_computation.11 | loop fusion | flops 2359296 | bytes 5242904 | tf_op jit(solution)/shard_map/add | solution.py:68
  30.5 0.8 multiply_bitcast_fusion
  31.3 0.2 multiply_subtract_fusion.1
  31.6 0.5 copy-done.2
  32.0 0.3 copy-done
  32.4 0.8 pad_maximum_fusion.15
  33.2 1.3 %collective-permute-start.2 = (f32[2,4,1,256]{3,1,2,0:T(4,128)S(1)}, f32[2,4,1,256]{3,1,2,0:T(4,128)S(1)}, u32[]{:S(2)}, u32[]{:S(2)}) collective-permute-start(f32[2,4,1,256]{3,1,2,0:T(4,128)S(1)} %copy.252), channel_id=1, source_target_pairs={{0,1},{2,3},{4,5},{6,7},{8,9},{10,11},{12,13},{14,15},{16,17},{18,... | collective-permute-start | bytes 24584 | tf_op jit(solution)/shard_map/ppermute | solution.py:20
  34.5 4.5 %collective-permute-start.3 = (f32[2,4,1,256]{3,1,2,0:T(4,128)S(1)}, f32[2,4,1,256]{3,1,2,0:T(4,128)S(1)}, u32[]{:S(2)}, u32[]{:S(2)}) collective-permute-start(f32[2,4,1,256]{3,1,2,0:T(4,128)S(1)} %copy.253), channel_id=1, source_target_pairs={{1,0},{3,2},{5,4},{7,6},{9,8},{11,10},{13,12},{15,14},{17,16},{19,... | collective-permute-start | bytes 24584 | tf_op jit(solution)/shard_map/ppermute | solution.py:21
  39.1 1.1 broadcast_multiply_fusion.1
  40.2 0.9 copy.261
  41.1 1.9 %mul.296 = f32[2,128,256]{2,1,0:T(8,128)} reshape(f32[2,128,2,128]{3,2,1,0:T(2,128)} %bitcast.85) | data formatting | bytes 524288 | tf_op jit(solution)/shard_map/mul | solution.py:144
  43.0 1.7 %select_maximum_fusion = f32[2,4,130,258]{3,2,1,0:T(8,128)S(1)} fusion(f32[2,4,1,256]{3,2,1,0:T(1,128)S(1)} %copy.255, f32[2,4,1,256]{3,2,1,0:T(1,128)S(1)} %copy.254, f32[2,1,128,256]{3,2,1,0:T(8,128)} %collective-permute-done.1, f32[2,1,128,256]{3,2,1,0:T(8,128)} %collective-permute-done, f32[1,2,128,256]{3,2,1,0:T(8,128)} %add_bitcast_fusion, ...), kind=kLoop, calls=%fused_computation.2 | loop fusion | flops 3756480 | bytes 2138240 | tf_op jit(solution)/shard_map/concatenate | solution.py:22
  44.8 0.8 copy-done.6
  45.7 0.9 fusion.32
  46.7 1.9 %collective-permute-start.4 = (f32[1,128,256]{2,1,0:T(8,128)S(1)}, f32[1,128,256]{2,1,0:T(8,128)S(1)}, u32[]{:S(2)}, u32[]{:S(2)}) collective-permute-start(f32[1,128,256]{2,1,0:T(8,128)S(1)} %get-tuple-element.87), channel_id=1, source_target_pairs={{2,0},{4,2},{6,4},{8,6},{10,8},{12,10},{14,12},{16,14},{18,16},{20... | collective-permute-start | bytes 393224 | tf_op jit(solution)/shard_map/ppermute | solution.py:21
  48.6 2.4 %collective-permute-start.5 = (f32[1,128,256]{2,1,0:T(8,128)S(1)}, f32[1,128,256]{2,1,0:T(8,128)S(1)}, u32[]{:S(2)}, u32[]{:S(2)}) collective-permute-start(f32[1,128,256]{2,1,0:T(8,128)S(1)} %get-tuple-element.86), channel_id=1, source_target_pairs={{0,2},{2,4},{4,6},{6,8},{8,10},{10,12},{12,14},{14,16},{16,18},{18... | collective-permute-start | bytes 393224 | tf_op jit(solution)/shard_map/ppermute | solution.py:20
  51.0 0.7 fusion.44
  51.7 0.7 fusion.45
  52.4 3.4 %collective-permute-done.5 = f32[1,128,256]{2,1,0:T(8,128)S(1)} collective-permute-done((f32[1,128,256]{2,1,0:T(8,128)S(1)}, f32[1,128,256]{2,1,0:T(8,128)S(1)}, u32[]{:S(2)}, u32[]{:S(2)}) %collective-permute-start.5) | collective-permute-done | bytes 131104 | tf_op jit(solution)/shard_map/ppermute | solution.py:20
  55.8 1.6 %collective-permute-start.6 = (f32[4,1,256]{2,1,0:T(1,128)S(1)}, f32[4,1,256]{2,1,0:T(1,128)S(1)}, u32[]{:S(2)}, u32[]{:S(2)}) collective-permute-start(f32[4,1,256]{2,1,0:T(1,128)S(1)} %get-tuple-element.83), channel_id=1, source_target_pairs={{1,0},{3,2},{5,4},{7,6},{9,8},{11,10},{13,12},{15,14},{17,16},{19,... | collective-permute-start | bytes 12296 | tf_op jit(solution)/shard_map/ppermute | solution.py:21
  57.4 1.3 %collective-permute-start.7 = (f32[4,1,256]{2,1,0:T(1,128)S(1)}, f32[4,1,256]{2,1,0:T(1,128)S(1)}, u32[]{:S(2)}, u32[]{:S(2)}) collective-permute-start(f32[4,1,256]{2,1,0:T(1,128)S(1)} %get-tuple-element.82), channel_id=1, source_target_pairs={{0,1},{2,3},{4,5},{6,7},{8,9},{10,11},{12,13},{14,15},{16,17},{18,... | collective-permute-start | bytes 12296 | tf_op jit(solution)/shard_map/ppermute | solution.py:20
  58.8 11.5 %subtract_maximum_fusion = (f32[2,256,128]{2,1,0:T(8,128)}, f32[2,256,128]{2,1,0:T(8,128)}, pred[2,256,128]{2,1,0:T(8,128)(4,1)S(1)}, pred[2,256,128]{2,1,0:T(8,...) fusion(f32[]{:T(128)} %bitcast.43, f32[]{:T(128)} %bitcast.42, ...), kind=kLoop, calls=%fused_computation.114 | loop fusion | flops 4063232 | bytes 3145792 | tf_op jit(solution)/shard_map/max | solution.py:88
  70.3 0.3 select_maximum_fusion.5
  70.7 0.8 fusion.21
  71.5 0.7 copy-done.10
  72.2 0.8 copy.256
  73.0 6.2 %all-to-all-start.1 = ((f32[2,128,256]{1,0,2:T(2,128)}), f32[2,128,256]{1,0,2:T(2,128)S(1)}, u32[]{:S(2)}, u32[]{:S(2)}) async-start(f32[2,128,256]{1,0,2:T(2,128)} %copy.256), calls=%async_computation.1 | async-start | bytes 524288 | tf_op jit(solution)/shard_map/all_to_all | solution.py:151
  79.2 11.2 %fusion.10 = f32[2,256,128]{2,1,0:T(8,128)S(1)} fusion(f32[1,2,256,128]{3,2,1,0:T(8,128)S(1)} %copy-done.5, pred[2,256,128]{2,1,0:T(8,128)(4,1)} %get-tuple-element.59, f32[]{:T(128)} %bitcast.43, pred[2,256,128]{2,1,0:T(8,128)(4,1)} %get-tuple-element.58, f32[]{:T(128)} %bitcast.42, pred[2,256,128]{2,1,0:T(8,128)(4,1)S(1)} %copy-done.15, f32[]{:T(128)} %bitcast.41, ...), kind=kLoop, calls=%fused_computation.56 | loop fusion | flops 2686976 | bytes 1310784 | tf_op jit(solution)/shard_map/div | solution.py:90
  90.8 1.6 %multiply_subtract_fusion = (f32[6,2,256,128]{3,2,1,0:T(8,128)S(1)}, f32[6,2,256,128]{3,2,1,0:T(8,128)}) fusion(f32[2,256,128]{2,1,0:T(8,128)S(1)} %bitcast.83, f32[6]{0:T(128)S(1)} %copy-done.18, f32[2,256,128]{2,1,0:T(8,128)S(1)} %fusion.10, f32[2,256,128]{2,1,0:T(8,128)S(1)} %copy-done.7, f32[6,2,256,128]{3,2,1,0:T(8,128)S(1)} %multiply_add_fusion.1, ...), kind=kLoop, calls=%fused_computation.8 | loop fusion | flops 2752512 | bytes 5767192 | tf_op jit(solution)/shard_map/sub | solution.py:95
  92.5 0.2 add_multiply_fusion.7
  92.8 0.2 add_multiply_fusion
  93.0 0.2 add_multiply_fusion.4
  93.4 0.7 slice_reduce_fusion
  94.2 1.3 %collective-permute-start.8 = (f32[3,3,256]{2,1,0:T(4,128)S(1)}, f32[3,3,256]{2,1,0:T(4,128)S(1)}, u32[]{:S(2)}, u32[]{:S(2)}) collective-permute-start(f32[3,3,256]{2,1,0:T(4,128)S(1)} %slice_reduce_fusion), channel_id=1, source_target_pairs={{0,1},{2,3},{4,5},{6,7},{8,9},{10,11},{12,13},{14,15},{16,17},{18,... | collective-permute-start | bytes 27656 | tf_op jit(solution)/shard_map/ppermute | solution.py:29
  95.5 0.5 fusion.3
  96.0 3.8 %collective-permute-done.8 = f32[3,3,256]{2,1,0:T(4,128)S(1)} collective-permute-done((f32[3,3,256]{2,1,0:T(4,128)S(1)}, f32[3,3,256]{2,1,0:T(4,128)S(1)}, u32[]{:S(2)}, u32[]{:S(2)}) %collective-permute-start.8) | collective-permute-done | bytes 9248 | tf_op jit(solution)/shard_map/ppermute | solution.py:29
  99.7 0.4 copy.258
  100.3 7.5 %scatter-add.6 = f32[3,3,256,128]{3,2,1,0:T(8,128)S(1)} dynamic-update-slice(f32[3,3,256,128]{3,2,1,0:T(8,128)S(1)} %fusion.3, f32[3,3,256,1]{3,2,1,0:T(8,128)S(1)} %slice_add_fusion, s32[]{:T(128)} %constant.100.clone.1, s32[]{:T(128)} %constant.100.clone.1, s32[]{:T(128)} %constant.100.clone.1, s32[]{:T(128)} %constant.100.clone.1) | dynamic-update-slice | bytes 18436 | tf_op jit(solution)/shard_map/scatter-add | solution.py:155
  107.8 1.9 %collective-permute-start.9 = (f32[3,256,128]{2,1,0:T(8,128)S(1)}, f32[3,256,128]{2,1,0:T(8,128)S(1)}, u32[]{:S(2)}, u32[]{:S(2)}) collective-permute-start(f32[3,256,128]{2,1,0:T(8,128)S(1)} %slice_bitcast_fusion.2), channel_id=1, source_target_pairs={{0,2},{2,4},{4,6},{6,8},{8,10},{10,12},{12,14},{14,16},{16,18},{18... | collective-permute-start | bytes 1179656 | tf_op jit(solution)/shard_map/ppermute | solution.py:29
  109.7 8.1 %collective-permute-done.9 = f32[3,256,128]{2,1,0:T(8,128)S(1)} collective-permute-done((f32[3,256,128]{2,1,0:T(8,128)S(1)}, f32[3,256,128]{2,1,0:T(8,128)S(1)}, u32[]{:S(2)}, u32[]{:S(2)}) %collective-permute-start.9) | collective-permute-done | bytes 393248 | tf_op jit(solution)/shard_map/ppermute | solution.py:29
  117.9 0.9 slice.475
  (60 shorter events, 1.4 us)
Async XLA Ops:
  0.6 22.5 %copy-start.1 = (f32[6,2,256,128]{3,2,1,0:T(8,128)S(1)}, f32[6,2,256,128]{3,2,1,0:T(8,128)}, u32[]{:S(2)}) copy-start(f32[6,2,256,128]{3,2,1,0:T(8,128)} %param.15) | copy-start | bytes 4718596
  16.5 12.2 %copy-start.18 = (f32[6]{0:T(128)S(1)}, f32[6]{0:T(128)}, u32[]{:S(2)}) copy-start(f32[6]{0:T(128)} %constant.126.clone) | copy-start | bytes 76
  16.5 15.5 %collective-permute-start = (f32[2,1,128,256]{3,2,1,0:T(8,128)}, f32[2,1,128,256]{3,2,1,0:T(8,128)}, u32[]{:S(2)}, u32[]{:S(2)}) collective-permute-start(f32[2,1,128,256]{3,2,1,0:T(8,128)} %get-tuple-element.84), channel_id=1, source_target_pairs={{0,2},{2,4},{4,6},{6,8},{8,10},{10,12},{12,14},{14,16},{16,18},{18... | collective-permute-start | bytes 786440 | tf_op jit(solution)/shard_map/ppermute | solution.py:20
  18.6 13.5 %collective-permute-start.1 = (f32[2,1,128,256]{3,2,1,0:T(8,128)}, f32[2,1,128,256]{3,2,1,0:T(8,128)}, u32[]{:S(2)}, u32[]{:S(2)}) collective-permute-start(f32[2,1,128,256]{3,2,1,0:T(8,128)} %get-tuple-element.85), channel_id=1, source_target_pairs={{2,0},{4,2},{6,4},{8,6},{10,8},{12,10},{14,12},{16,14},{18,16},{20... | collective-permute-start | bytes 786440 | tf_op jit(solution)/shard_map/ppermute | solution.py:21
  24.1 14.9 %all-to-all-start = ((f32[2,256,128]{2,0,1:T(2,128)}), f32[2,256,128]{2,0,1:T(2,128)}, u32[]{:S(2)}, u32[]{:S(2)}) async-start(f32[2,256,128]{2,0,1:T(2,128)} %copy.250), calls=%async_computation | async-start | bytes 524288 | tf_op jit(solution)/shard_map/all_to_all | solution.py:141
  31.3 0.7 copy-start.2
  31.3 1.0 copy-start
  33.2 9.7 %collective-permute-start.2 = (f32[2,4,1,256]{3,1,2,0:T(4,128)S(1)}, f32[2,4,1,256]{3,1,2,0:T(4,128)S(1)}, u32[]{:S(2)}, u32[]{:S(2)}) collective-permute-start(f32[2,4,1,256]{3,1,2,0:T(4,128)S(1)} %copy.252), channel_id=1, source_target_pairs={{0,1},{2,3},{4,5},{6,7},{8,9},{10,11},{12,13},{14,15},{16,17},{18,... | collective-permute-start | bytes 24584 | tf_op jit(solution)/shard_map/ppermute | solution.py:20
  34.5 8.4 %collective-permute-start.3 = (f32[2,4,1,256]{3,1,2,0:T(4,128)S(1)}, f32[2,4,1,256]{3,1,2,0:T(4,128)S(1)}, u32[]{:S(2)}, u32[]{:S(2)}) collective-permute-start(f32[2,4,1,256]{3,1,2,0:T(4,128)S(1)} %copy.253), channel_id=1, source_target_pairs={{1,0},{3,2},{5,4},{7,6},{9,8},{11,10},{13,12},{15,14},{17,16},{19,... | collective-permute-start | bytes 24584 | tf_op jit(solution)/shard_map/ppermute | solution.py:21
  44.7 1.0 copy-start.6
  44.7 1.0 copy-start.9
  45.7 5.3 %copy-start.16 = (f32[8]{0:T(128)S(1)}, f32[8]{0:T(128)}, u32[]{:S(2)}) copy-start(f32[8]{0:T(128)} %param.19) | copy-start | bytes 100
  45.7 6.0 %copy-start.17 = (f32[8]{0:T(128)S(1)}, f32[8]{0:T(128)}, u32[]{:S(2)}) copy-start(f32[8]{0:T(128)} %param.18) | copy-start | bytes 100
  45.7 13.0 %copy-start.4 = (f32[1,2,256,128]{3,2,1,0:T(8,128)S(1)}, f32[1,2,256,128]{3,2,1,0:T(8,128)}, u32[]{:S(2)}) copy-start(f32[1,2,256,128]{3,2,1,0:T(8,128)} %get-tuple-element.61) | copy-start | bytes 786436
  45.7 13.0 %copy-start.11 = (s32[2,256,128]{2,1,0:T(8,128)S(1)}, s32[2,256,128]{2,1,0:T(8,128)}, u32[]{:S(2)}) copy-start(s32[2,256,128]{2,1,0:T(8,128)} %param.17) | copy-start | bytes 786436
  46.7 5.7 %collective-permute-start.4 = (f32[1,128,256]{2,1,0:T(8,128)S(1)}, f32[1,128,256]{2,1,0:T(8,128)S(1)}, u32[]{:S(2)}, u32[]{:S(2)}) collective-permute-start(f32[1,128,256]{2,1,0:T(8,128)S(1)} %get-tuple-element.87), channel_id=1, source_target_pairs={{2,0},{4,2},{6,4},{8,6},{10,8},{12,10},{14,12},{16,14},{18,16},{20... | collective-permute-start | bytes 393224 | tf_op jit(solution)/shard_map/ppermute | solution.py:21
  48.6 7.2 %collective-permute-start.5 = (f32[1,128,256]{2,1,0:T(8,128)S(1)}, f32[1,128,256]{2,1,0:T(8,128)S(1)}, u32[]{:S(2)}, u32[]{:S(2)}) collective-permute-start(f32[1,128,256]{2,1,0:T(8,128)S(1)} %get-tuple-element.86), channel_id=1, source_target_pairs={{0,2},{2,4},{4,6},{6,8},{8,10},{10,12},{12,14},{14,16},{16,18},{18... | collective-permute-start | bytes 393224 | tf_op jit(solution)/shard_map/ppermute | solution.py:20
  55.8 14.5 %collective-permute-start.6 = (f32[4,1,256]{2,1,0:T(1,128)S(1)}, f32[4,1,256]{2,1,0:T(1,128)S(1)}, u32[]{:S(2)}, u32[]{:S(2)}) collective-permute-start(f32[4,1,256]{2,1,0:T(1,128)S(1)} %get-tuple-element.83), channel_id=1, source_target_pairs={{1,0},{3,2},{5,4},{7,6},{9,8},{11,10},{13,12},{15,14},{17,16},{19,... | collective-permute-start | bytes 12296 | tf_op jit(solution)/shard_map/ppermute | solution.py:21
  57.4 12.8 %collective-permute-start.7 = (f32[4,1,256]{2,1,0:T(1,128)S(1)}, f32[4,1,256]{2,1,0:T(1,128)S(1)}, u32[]{:S(2)}, u32[]{:S(2)}) collective-permute-start(f32[4,1,256]{2,1,0:T(1,128)S(1)} %get-tuple-element.82), channel_id=1, source_target_pairs={{0,1},{2,3},{4,5},{6,7},{8,9},{10,11},{12,13},{14,15},{16,17},{18,... | collective-permute-start | bytes 12296 | tf_op jit(solution)/shard_map/ppermute | solution.py:20
  70.6 8.6 %copy-start.5 = (f32[1,2,256,128]{3,2,1,0:T(8,128)S(1)}, f32[1,2,256,128]{3,2,1,0:T(8,128)}, u32[]{:S(2)}) copy-start(f32[1,2,256,128]{3,2,1,0:T(8,128)} %get-tuple-element.61) | copy-start | bytes 786436
  70.6 8.6 %copy-start.8 = (f32[2,256,128]{2,1,0:T(8,128)S(1)}, f32[2,256,128]{2,1,0:T(8,128)}, u32[]{:S(2)}) copy-start(f32[2,256,128]{2,1,0:T(8,128)} %get-tuple-element.51) | copy-start | bytes 786436
  70.6 8.6 %copy-start.12 = (pred[2,256,128]{2,1,0:T(8,128)(4,1)S(1)}, pred[2,256,128]{2,1,0:T(8,128)(4,1)}, u32[]{:S(2)}) copy-start(pred[2,256,128]{2,1,0:T(8,128)(4,1)} %get-tuple-element.54) | copy-start | bytes 196612
  70.6 8.6 %copy-start.13 = (pred[2,256,128]{2,1,0:T(8,128)(4,1)S(1)}, pred[2,256,128]{2,1,0:T(8,128)(4,1)}, u32[]{:S(2)}) copy-start(pred[2,256,128]{2,1,0:T(8,128)(4,1)} %get-tuple-element.55) | copy-start | bytes 196612
  70.6 8.6 %copy-start.14 = (pred[2,256,128]{2,1,0:T(8,128)(4,1)S(1)}, pred[2,256,128]{2,1,0:T(8,128)(4,1)}, u32[]{:S(2)}) copy-start(pred[2,256,128]{2,1,0:T(8,128)(4,1)} %get-tuple-element.56) | copy-start | bytes 196612
  70.7 8.6 %copy-start.15 = (pred[2,256,128]{2,1,0:T(8,128)(4,1)S(1)}, pred[2,256,128]{2,1,0:T(8,128)(4,1)}, u32[]{:S(2)}) copy-start(pred[2,256,128]{2,1,0:T(8,128)(4,1)} %get-tuple-element.57) | copy-start | bytes 196612
  71.5 0.7 copy-start.10
  73.0 17.7 %copy-start.3 = (f32[2,256,128]{2,1,0:T(8,128)S(1)}, f32[2,256,128]{2,1,0:T(8,128)}, u32[]{:S(2)}) copy-start(f32[2,256,128]{2,1,0:T(8,128)} %copy-done.2) | copy-start | bytes 786436
  73.0 17.7 %copy-start.7 = (f32[2,256,128]{2,1,0:T(8,128)S(1)}, f32[2,256,128]{2,1,0:T(8,128)}, u32[]{:S(2)}) copy-start(f32[2,256,128]{2,1,0:T(8,128)} %get-tuple-element.50) | copy-start | bytes 786436
  73.0 17.4 %all-to-all-start.1 = ((f32[2,128,256]{1,0,2:T(2,128)}), f32[2,128,256]{1,0,2:T(2,128)S(1)}, u32[]{:S(2)}, u32[]{:S(2)}) async-start(f32[2,128,256]{1,0,2:T(2,128)} %copy.256), calls=%async_computation.1 | async-start | bytes 524288 | tf_op jit(solution)/shard_map/all_to_all | solution.py:151
  94.2 5.6 %collective-permute-start.8 = (f32[3,3,256]{2,1,0:T(4,128)S(1)}, f32[3,3,256]{2,1,0:T(4,128)S(1)}, u32[]{:S(2)}, u32[]{:S(2)}) collective-permute-start(f32[3,3,256]{2,1,0:T(4,128)S(1)} %slice_reduce_fusion), channel_id=1, source_target_pairs={{0,1},{2,3},{4,5},{6,7},{8,9},{10,11},{12,13},{14,15},{16,17},{18,... | collective-permute-start | bytes 27656 | tf_op jit(solution)/shard_map/ppermute | solution.py:29
  107.8 10.0 %collective-permute-start.9 = (f32[3,256,128]{2,1,0:T(8,128)S(1)}, f32[3,256,128]{2,1,0:T(8,128)S(1)}, u32[]{:S(2)}, u32[]{:S(2)}) collective-permute-start(f32[3,256,128]{2,1,0:T(8,128)S(1)} %slice_bitcast_fusion.2), channel_id=1, source_target_pairs={{0,2},{2,4},{4,6},{6,8},{8,10},{10,12},{12,14},{14,16},{16,18},{18... | collective-permute-start | bytes 1179656 | tf_op jit(solution)/shard_map/ppermute | solution.py:29
where the time goes:
time: 120 us; the launch traced here: 119 us
  other arithmetic  48.5 us (40%)
  starting transfers between devices  33.7 us (28%)
  local copies, waits for them, and re-layouts  20.2 us (17%)
  waiting for transfers between devices  15.3 us (13%)
    another operation x2, other arithmetic, on_device(): jnp.stack([pressure, conduct])  13.9 us
    ppermute x4, starting transfers between devices, extended(): after = lax.ppermute(leading, axis, down)  12.6 us
    ppermute x2, waiting for transfers between devices, passed_along(): return lax.ppermute(block, axis, route)  11.9 us
    max x1, other arithmetic, plastic(): jnp.maximum(1.0 - SHEAR * multiplier / jnp.maximum(equiv_shear, FLOOR), 0.0)  11.5 us
    div x1, other arithmetic, plastic(): return deviator * shrink_factor + normal_mask * (new_invariant / 3.0)  11.2 us
    scatter-add x1, local copies, waits for them, and re-layouts, on_device(): node_main = node_main.at[:, :, :, 0].add(from_below)  7.48 us
    ppermute x4, starting transfers between devices, extended(): before = lax.ppermute(last, axis, up)  7.03 us
    all_to_all x1, starting transfers between devices, on_device(): lax.all_to_all(pressure_next, 'gz', split_axis=2, concat_axis=1, tiled=True)  6.2 us
  transfers between devices with their start and end apart: 12, of which 3 were waited for; matrix products, arithmetic and copies ran while one was open for 28% of the time, Pallas kernels for 0%

commit v1 on v0

v1 whole, which is shorter than its diff:
```python
import functools

import jax
import jax.numpy as jnp
from jax import lax
from jax.experimental import pallas as pl
from jax.experimental.pallas import tpu as pltpu
from jax.sharding import PartitionSpec as P

MESH = pl.DeviceIdType.MESH
LANES = 128
PAD = 8
ROWS = 8
F32 = jnp.float32


def pick(ids, tables):
    levels = [list(t) for t in tables]
    bit = 1
    while len(levels[0]) > 1:
        odd = (ids & bit) != 0
        levels = [
            [jnp.where(odd, t[2 * j + 1], t[2 * j]) for j in range(len(t) // 2)] for t in levels
        ]
        bit *= 2
    return levels


def kernel(
    n,
    count,
    e_hbm,
    s_hbm,
    m_hbm,
    coh,
    fri,
    p_hbm,
    st_hbm,
    c_hbm,
    ptab,
    pn_hbm,
    so_hbm,
    f_hbm,
    E,
    S,
    M,
    SR,
    RF,
    PK,
    C,
    ST,
    HX,
    F1,
    HF,
    CO,
    CX,
    PN,
    EP,
    PM,
    EM,
    T,
    FS,
    SL,
    SLR,
    RM,
    RMR,
    OUTP,
    loc,
    snd,
    rcv,
):
    g = lax.axis_index("gx")
    h = lax.axis_index("gz")
    ym = SR.shape[1]
    ny = RF.shape[2]
    sem_at = [0, 0]
    rows_of = lambda who: pl.ds(pl.multiple_of(who * ny, 8), ny)
    prow_of = lambda who: pl.ds(pl.multiple_of(PAD + who * ny, 8), ny)

    def local(src, dst):
        k = sem_at[0]
        sem_at[0] += 1
        return pltpu.make_async_copy(src, dst, loc.at[k])

    def remote(src, dst, gx, gz):
        k = sem_at[1]
        sem_at[1] += 1
        return pltpu.make_async_remote_copy(
            src_ref=src,
            dst_ref=dst,
            send_sem=snd.at[k],
            recv_sem=rcv.at[k],
            device_id=(gx, gz),
            device_id_type=MESH,
        )

    has_lo, has_hi = g > 0, g < count - 1
    ld_p = [local(p_hbm.at[:, :, pl.ds(c * LANES, LANES)], PK.at[0, c, :, pl.ds(PAD, ny)]) for c in range(n)]
    ld_c = [local(c_hbm.at[:, :, pl.ds(c * LANES, LANES)], C.at[c]) for c in range(n)]
    ld_e = local(e_hbm.at[pl.ds(0, 3)], E.at[pl.ds(0, 3)])
    ld_e2 = local(e_hbm.at[pl.ds(3, 3)], E.at[pl.ds(3, 3)])
    ld_s = local(s_hbm, S)
    ld_m = local(m_hbm, M)
    ld_st = [local(st_hbm.at[:, :, pl.ds(c * LANES, LANES)], ST.at[c]) for c in range(n)]
    for cp in [ld_e] + ld_c + ld_p + [ld_m, ld_e2, ld_s] + ld_st:
        cp.start()

    PK[:, :, :, 0:PAD, :] = jnp.zeros((2, n, 2, PAD, LANES), F32)
    PK[:, :, :, PAD + ny : 2 * PAD + ny, :] = jnp.zeros((2, n, 2, PAD, LANES), F32)
    F1[:, :, 0:PAD, :] = jnp.zeros((n, 2, PAD, LANES), F32)
    F1[:, :, PAD + ny : 2 * PAD + ny, :] = jnp.zeros((n, 2, PAD, LANES), F32)

    @pl.when(jnp.logical_not(has_lo))
    def _():
        HX[0] = jnp.zeros(HX.shape[1:], F32)
        HF[0] = jnp.zeros(HF.shape[1:], F32)
        PM[0] = jnp.zeros(PM.shape[1:], F32)
        EM[0] = jnp.zeros(EM.shape[1:], F32)
        SLR[...] = jnp.zeros(SLR.shape, F32)

    @pl.when(jnp.logical_not(has_hi))
    def _():
        HX[1] = jnp.zeros(HX.shape[1:], F32)
        HF[1] = jnp.zeros(HF.shape[1:], F32)

    @pl.when(h == 0)
    def _():
        EM[...] = jnp.zeros(EM.shape, F32)
        RMR[...] = jnp.zeros(RMR.shape, F32)

    PM[:, 0:PAD, :] = jnp.zeros((3, PAD, LANES), F32)
    EM[:, 0:PAD, :] = jnp.zeros((2, PAD, LANES), F32)
    T[:, :, 0:PAD, :] = jnp.zeros((6, 2, PAD, LANES), F32)

    barrier = pltpu.get_barrier_semaphore()
    for d in range(1, n):
        pl.semaphore_signal(barrier, inc=1, device_id=(g, lax.rem(h + d, n)), device_id_type=MESH)

    @pl.when(has_lo)
    def _():
        for d in range(n):
            pl.semaphore_signal(barrier, inc=1, device_id=(g - 1, lax.rem(h + d, n)), device_id_type=MESH)

    @pl.when(has_hi)
    def _():
        for d in range(n):
            pl.semaphore_signal(barrier, inc=1, device_id=(g + 1, lax.rem(h + d, n)), device_id_type=MESH)

    ld_e.wait()

    def rate_step(i, _):
        rows = pl.ds(pl.multiple_of(i * 16, 16), 16)
        SR[:, rows, :] = E[0, :, rows, :] + E[1, :, rows, :] + E[2, :, rows, :]
        return 0

    lax.fori_loop(0, ym // 16, rate_step, 0)
    for cp in ld_c:
        cp.wait()
    ptable = [ptab[j] for j in range(ptab.shape[0])]

    def cond_step(i, _):
        rows = pl.ds(pl.multiple_of(i * ROWS, ROWS), ROWS)
        for c in range(n):
            PK[1, c, :, pl.ds(pl.multiple_of(PAD + i * ROWS, ROWS), ROWS), :] = pick(
                C[c, :, rows, :], [ptable]
            )[0][0]
        return 0

    lax.fori_loop(0, ny // ROWS, cond_step, 0)
    for cp in ld_p:
        cp.wait()

    pl.semaphore_wait(barrier, (n - 1) + n * has_lo.astype(jnp.int32) + n * has_hi.astype(jnp.int32))

    rates = []
    for d in range(1, n):
        to = lax.rem(h + d, n)
        rates.append(remote(SR.at[:, rows_of(to), :], RF.at[h], g, to))
        rates[-1].start()
    both = pl.ds(0, 2)
    chunks = pl.ds(0, n)
    inner = pl.ds(PAD, ny)
    lo_x = remote(PK.at[both, chunks, 0, inner], HX.at[1], g - 1, h)
    hi_x = remote(PK.at[both, chunks, 1, inner], HX.at[0], g + 1, h)
    lo_y = remote(PK.at[:, :, :, pl.ds(PAD, PAD)], PK.at[:, :, :, pl.ds(PAD + ny, PAD)], g, h - 1)
    hi_y = remote(PK.at[:, :, :, pl.ds(ny, PAD)], PK.at[:, :, :, pl.ds(0, PAD)], g, h + 1)
    lo_f = remote(F1.at[chunks, 0, inner], HF.at[1], g - 1, h)
    hi_f = remote(F1.at[chunks, 1, inner], HF.at[0], g + 1, h)
    lo_fy = remote(F1.at[:, :, pl.ds(PAD, PAD)], F1.at[:, :, pl.ds(PAD + ny, PAD)], g, h - 1)
    hi_fy = remote(F1.at[:, :, pl.ds(ny, PAD)], F1.at[:, :, pl.ds(0, PAD)], g, h + 1)
    rim = remote(RM, RMR, g, h + 1)
    slab = remote(SL, SLR, g + 1, h)

    def begin(lo, hi, at, size):
        @pl.when(at > 0)
        def _():
            lo.start()

        @pl.when(at < size - 1)
        def _():
            hi.start()

    def arrive(lo, hi, at, size):
        @pl.when(at > 0)
        def _():
            hi.wait_recv()

        @pl.when(at < size - 1)
        def _():
            lo.wait_recv()

    def sent(lo, hi, at, size):
        @pl.when(at > 0)
        def _():
            lo.wait_send()

        @pl.when(at < size - 1)
        def _():
            hi.wait_send()

    begin(lo_x, hi_x, g, count)
    begin(lo_y, hi_y, h, n)
    RF[h] = SR[:, rows_of(h), :]

    ld_e2.wait()
    ld_s.wait()
    ld_m.wait()
    ctable = [coh[j] for j in range(coh.shape[0])]
    ftable = [fri[j] for j in range(fri.shape[0])]

    def plastic_step(i, _):
        rows = pl.ds(pl.multiple_of(i * ROWS, ROWS), ROWS)
        prow = pl.ds(pl.multiple_of(PAD + i * ROWS, ROWS), ROWS)
        vol = SR[:, rows, :]
        base = 1.5 * vol - 2.0 * (vol * (1.0 / 3.0))
        t = [S[c, :, rows, :] + 2.0 * E[c, :, rows, :] for c in range(6)]
        t = [t[0] + base, t[1] + base, t[2] + base] + t[3:]
        inv = t[0] + t[1] + t[2]
        third = inv * (1.0 / 3.0)
        dev = [t[0] - third, t[1] - third, t[2] - third] + t[3:]
        second = 0.5 * (dev[0] * dev[0] + dev[1] * dev[1] + dev[2] * dev[2])
        second = second + dev[3] * dev[3] + dev[4] * dev[4] + dev[5] * dev[5]
        q = jnp.sqrt(second)
        (strength,), (slope,) = pick(M[:, rows, :], [ctable, ftable])
        over = jnp.maximum(q + slope * inv - strength, 0.0)
        floor = jnp.maximum(q, 0.25)
        ratio = over / ((1.0 + 13.5 * slope * slope) * floor)
        shrink = jnp.maximum(1.0 - ratio, 0.0)
        mean = (inv - 13.5 * slope * (ratio * floor)) * (1.0 / 3.0)
        for c in range(6):
            out = dev[c] * shrink
            T[c, :, prow, :] = out + mean if c < 3 else out
        return 0

    lax.fori_loop(0, ym // ROWS, plastic_step, 0)
    st_out = local(T.at[:, :, pl.ds(PAD, ym)], so_hbm)
    st_out.start()

    lane = lax.broadcasted_iota(jnp.int32, (ROWS, LANES), 1)
    first = lane == 0
    final_lane = lane == LANES - 1
    zero = jnp.zeros((ROWS, LANES), F32)
    XC, YC, ZC = (0, 3, 5), (3, 1, 4), (5, 4, 2)

    def force_step(i, _):
        rows = pl.ds(pl.multiple_of(i * ROWS, ROWS), ROWS)
        prow = pl.ds(pl.multiple_of(PAD + i * ROWS, ROWS), ROWS)
        urow = pl.ds(PAD - 1 + i * ROWS, ROWS)
        main, side = [], []
        for a in range(2):
            s_now, d_now, s_up, d_up, r_now, r_up = [], [], [], [], [], []
            for c in range(6):
                t, u = T[c, a, prow, :], T[c, a, urow, :]
                tr, ur = pltpu.roll(t, 1, 1), pltpu.roll(u, 1, 1)
                tz, uz = jnp.where(first, 0.0, tr), jnp.where(first, 0.0, ur)
                s_now.append(t + tz)
                d_now.append(tz - t)
                s_up.append(u + uz)
                d_up.append(uz - u)
                r_now.append(tr)
                r_up.append(ur)
            line, edge = [], []
            for r in range(3):
                x, y, z = XC[r], YC[r], ZC[r]
                u_r = s_now[x] + s_up[x]
                v_r = (s_up[y] - s_now[y]) + (d_now[z] + d_up[z])
                line.append((0.25 * (v_r - u_r), 0.25 * (v_r + u_r)))
                u_r = r_now[x] + r_up[x]
                v_r = (r_up[y] - r_now[y]) + (r_now[z] + r_up[z])
                edge.append((0.25 * (v_r - u_r), 0.25 * (v_r + u_r)))
            main.append(line)
            side.append(edge)
        packed = zero
        for r in range(3):
            FS[r, 0, rows, :] = main[0][r][0]
            FS[r, 1, rows, :] = main[1][r][0] + main[0][r][1]
            SL[r, rows, :] = main[1][r][1]
            cols = [side[0][r][0], side[1][r][0] + side[0][r][1], side[1][r][1]]
            for j in range(3):
                at = 3 * j + r
                col = cols[j] if at == 0 else pltpu.roll(cols[j], at, 1)
                packed = jnp.where(lane == at, col, packed)
        RM[rows, :] = packed
        return 0

    lax.fori_loop(0, ym // ROWS, force_step, 0)

    @pl.when(h < n - 1)
    def _():
        rim.start()

    for cp in ld_st:
        cp.wait()
    for cp in rates:
        cp.wait_recv()
    arrive(lo_x, hi_x, g, count)
    arrive(lo_y, hi_y, h, n)

    def up_one(parts):
        turned = [pltpu.roll(x, LANES - 1, 1) for x in parts]
        return [jnp.where(final_lane, turned[c + 1] if c + 1 < n else 0.0, turned[c]) for c in range(n)]

    def down_one(parts):
        turned = [pltpu.roll(x, 1, 1) for x in parts]
        return [jnp.where(first, turned[c - 1] if c > 0 else 0.0, turned[c]) for c in range(n)]

    def face(a, b):
        return 2.0 * a * b / (a + b)

    def sweep_one(i, _):
        rows = pl.ds(pl.multiple_of(i * ROWS, ROWS), ROWS)
        prow = pl.ds(pl.multiple_of(PAD + i * ROWS, ROWS), ROWS)
        urow = pl.ds(PAD - 1 + i * ROWS, ROWS)
        drow = pl.ds(PAD + 1 + i * ROWS, ROWS)
        mids = []
        for a in range(2):
            k = [PK[1, c, a, prow, :] for c in range(n)]
            p = [PK[0, c, a, prow, :] for c in range(n)]
            tzp = [face(x, y) for x, y in zip(k, up_one(k))]
            tzm = down_one(tzp)
            pzp, pzm = up_one(p), down_one(p)
            for c in range(n):
                tym = face(k[c], PK[1, c, a, urow, :])
                typ = face(k[c], PK[1, c, a, drow, :])
                out = face(k[c], HX[a, 1, c, rows, :])
                if a == 0:
                    mids.append(face(k[c], PK[1, c, 1, prow, :]))
                    CX[0, c, rows, :] = mids[c]
                CX[1 + a, c, rows, :] = out
                st = ST[c, a, rows, :]
                source = st * p[c] - 0.8 * RF[c, a, rows, :]
                inverse = 1.0 / (st + out + mids[c] + tym + typ + tzm[c] + tzp[c])
                num = (
                    source
                    + out * HX[a, 0, c, rows, :]
                    + mids[c] * PK[0, c, 1 - a, prow, :]
                    + tym * PK[0, c, a, urow, :]
                    + typ * PK[0, c, a, drow, :]
                    + tzm[c] * pzm[c]
                    + tzp[c] * pzp[c]
                )
                for j, val in enumerate((tym, typ, tzm[c], tzp[c], inverse, source)):
                    CO[j, c, a, rows, :] = val
                F1[c, a, prow, :] = num * inverse
        return 0

    lax.fori_loop(0, ny // ROWS, sweep_one, 0)
    begin(lo_f, hi_f, g, count)
    begin(lo_fy, hi_fy, h, n)

    @pl.when(h > 0)
    def _():
        rim.wait_recv()

    def slab_step(i, _):
        rows = pl.ds(pl.multiple_of(i * ROWS, ROWS), ROWS)
        got = RMR[rows, :]
        for r in range(3):
            SL[r, rows, :] = SL[r, rows, :] + jnp.where(first, pltpu.roll(got, LANES - 6 - r, 1), 0.0)
        return 0

    lax.fori_loop(0, ym // ROWS, slab_step, 0)

    @pl.when(has_hi)
    def _():
        slab.start()

    arrive(lo_f, hi_f, g, count)
    arrive(lo_fy, hi_fy, h, n)

    def sweep_two(i, _):
        rows = pl.ds(pl.multiple_of(i * ROWS, ROWS), ROWS)
        prow = pl.ds(pl.multiple_of(PAD + i * ROWS, ROWS), ROWS)
        urow = pl.ds(PAD - 1 + i * ROWS, ROWS)
        drow = pl.ds(PAD + 1 + i * ROWS, ROWS)
        result = []
        for a in range(2):
            p = [F1[c, a, prow, :] for c in range(n)]
            pzp, pzm = up_one(p), down_one(p)
            line = []
            for c in range(n):
                tym, typ, tzm, tzp, inverse, source = (CO[j, c, a, rows, :] for j in range(6))
                num = (
                    source
                    + CX[1 + a, c, rows, :] * HF[a, c, rows, :]
                    + CX[0, c, rows, :] * F1[c, 1 - a, prow, :]
                    + tym * F1[c, a, urow, :]
                    + typ * F1[c, a, drow, :]
                    + tzm * pzm[c]
                    + tzp * pzp[c]
                )
                new = num * inverse
                PN[c, a, rows, :] = new
                OUTP[a, rows, pl.ds(c * LANES, LANES)] = new
                line.append(new)
            result.append(line)
        for c in range(1, n):
            left, right = pltpu.roll(result[0][c - 1], 1, 1), pltpu.roll(result[1][c - 1], 2, 1)
            EP[c, rows, :] = jnp.where(first, left, right)
        return 0

    lax.fori_loop(0, ny // ROWS, sweep_two, 0)

    mine, ahead = [], []
    for d in range(1, n):
        to = lax.rem(h + d, n)
        mine.append((to, remote(PN.at[to], PM.at[pl.ds(1, 2), prow_of(h)], g, to), remote(EP.at[to], EM.at[1, prow_of(h)], g, to)))
    for d in range(n):
        to = lax.rem(h + d, n)
        ahead.append((to, remote(PN.at[to, 1], PM.at[0, prow_of(h)], g + 1, to), remote(EP.at[to], EM.at[0, prow_of(h)], g + 1, to)))
    for to, body, brim in mine:
        body.start()

        @pl.when(to > 0)
        def _():
            brim.start()

    @pl.when(has_hi)
    def _():
        for to, body, brim in ahead:
            body.start()

            @pl.when(to > 0)
            def _():
                brim.start()

    pn_out = local(OUTP, pn_hbm)
    pn_out.start()
    PM[1:3, prow_of(h), :] = PN[h]

    @pl.when(h > 0)
    def _():
        EM[1, prow_of(h), :] = EP[h]

    @pl.when(has_lo)
    def _():
        slab.wait_recv()

    for to, body, brim in mine:
        body.wait_recv()

        @pl.when(h > 0)
        def _():
            brim.wait_recv()

    @pl.when(has_lo)
    def _():
        for to, body, brim in ahead:
            body.wait_recv()

            @pl.when(h > 0)
            def _():
                brim.wait_recv()

    def last_step(i, _):
        rows = pl.ds(pl.multiple_of(i * ROWS, ROWS), ROWS)
        prow = pl.ds(pl.multiple_of(PAD + i * ROWS, ROWS), ROWS)
        urow = pl.ds(PAD - 1 + i * ROWS, ROWS)
        got = RMR[rows, :]
        lines = []
        for j in range(3):
            parts = []
            for at in (prow, urow):
                p = PM[j, at, :]
                if j == 0:
                    edge = pltpu.roll(EM[0, at, :], LANES - 1, 1)
                elif j == 1:
                    edge = EM[1, at, :]
                else:
                    edge = pltpu.roll(EM[1, at, :], LANES - 1, 1)
                pz = jnp.where(first, edge, pltpu.roll(p, 1, 1))
                parts.append((p + pz, pz - p))
            (s0, d0), (s1, d1) = parts
            lines.append((s0 + s1, s1 - s0, d0 + d1))
        for j in range(2):
            (ss0, ds0, sd0), (ss1, ds1, sd1) = lines[j], lines[j + 1]
            pressure = (ss0 - ss1, ds0 + ds1, sd0 + sd1)
            for r in range(3):
                at = 3 * j + r
                col = got if at == 0 else pltpu.roll(got, LANES - at, 1)
                total = FS[r, j, rows, :] + jnp.where(first, col, 0.0) - 0.2 * pressure[r]
                if j == 0:
                    total = total + SLR[r, rows, :]
                FS[r, j, rows, :] = total
        return 0

    lax.fori_loop(0, ym // ROWS, last_step, 0)
    f_out = local(FS, f_hbm)
    f_out.start()

    for cp in rates:
        cp.wait_send()
    sent(lo_x, hi_x, g, count)
    sent(lo_y, hi_y, h, n)
    sent(lo_f, hi_f, g, count)
    sent(lo_fy, hi_fy, h, n)

    @pl.when(h < n - 1)
    def _():
        rim.wait_send()

    for to, body, brim in mine:
        body.wait_send()

        @pl.when(to > 0)
        def _():
            brim.wait_send()

    @pl.when(has_hi)
    def _():
        slab.wait_send()
        for to, body, brim in ahead:
            body.wait_send()

            @pl.when(to > 0)
            def _():
                brim.wait_send()

    st_out.wait()
    pn_out.wait()
    f_out.wait()


def on_device(n, count, *args):
    strain_inc, pressure = args[0], args[5]
    planes, ym = strain_inc.shape[1], strain_inc.shape[2]
    ny = pressure.shape[1]
    assert planes == 2 and strain_inc.shape[3] == LANES and pressure.shape[2] == n * LANES
    vm = lambda *shape: pltpu.VMEM(shape, F32)
    vi = lambda *shape: pltpu.VMEM(shape, jnp.int32)
    any_spec = pl.BlockSpec(memory_space=pl.ANY)
    smem = pl.BlockSpec(memory_space=pltpu.SMEM)
    loads = 3 * n + 7
    sends = (n - 1) + 10 + 2 * (n - 1) + 2 * n
    return pl.pallas_call(
        functools.partial(kernel, n, count),
        out_shape=(
            jax.ShapeDtypeStruct(pressure.shape, F32),
            jax.ShapeDtypeStruct(strain_inc.shape, F32),
            jax.ShapeDtypeStruct((3,) + strain_inc.shape[1:], F32),
        ),
        in_specs=[any_spec, any_spec, any_spec, smem, smem, any_spec, any_spec, any_spec, smem],
        out_specs=(any_spec, any_spec, any_spec),
        scratch_shapes=[
            vm(6, 2, ym, LANES),
            vm(6, 2, ym, LANES),
            vi(2, ym, LANES),
            vm(2, ym, LANES),
            vm(n, 2, ny, LANES),
            vm(2, n, 2, ny + 2 * PAD, LANES),
            vi(n, 2, ny, LANES),
            vm(n, 2, ny, LANES),
            vm(2, 2, n, ny, LANES),
            vm(n, 2, ny + 2 * PAD, LANES),
            vm(2, n, ny, LANES),
            vm(6, n, 2, ny, LANES),
            vm(3, n, ny, LANES),
            vm(n, 2, ny, LANES),
            vm(n, ny, LANES),
            vm(3, PAD + ym, LANES),
            vm(2, PAD + ym, LANES),
            vm(6, 2, PAD + ym, LANES),
            vm(3, 2, ym, LANES),
            vm(3, ym, LANES),
            vm(3, ym, LANES),
            vm(ym, LANES),
            vm(ym, LANES),
            vm(2, ny, n * LANES),
            pltpu.SemaphoreType.DMA((loads,)),
            pltpu.SemaphoreType.DMA((sends,)),
            pltpu.SemaphoreType.DMA((sends,)),
        ],
        compiler_params=pltpu.CompilerParams(
            collective_id=0, has_side_effects=True, vmem_limit_bytes=48 * 1024 * 1024
        ),
    )(*args)


def solution(mesh):
    in_specs = (
        P(None, "gx", None, "gz"),
        P(None, "gx", None, "gz"),
        P("gx", None, "gz"),
        P(),
        P(),
        P("gx", "gz", None),
        P("gx", "gz", None),
        P("gx", "gz", None),
        P(),
    )
    out_specs = (P("gx", "gz", None), P(None, "gx", None, "gz"), P(None, "gx", None, "gz"))
    return jax.shard_map(
        functools.partial(on_device, mesh.shape["gz"], mesh.shape["gx"]),
        mesh=mesh,
        in_specs=in_specs,
        out_specs=out_specs,
        check_vma=False,
    )
```

time: 120 us -> 44.4 us (0.37)
  the two profiles are of different devices: /device:TPU:10 before, /device:TPU:14 now
where the time goes in v1:
time: 44.4 us; the launch traced here: 44.1 us
  Pallas kernels  33.5 us (75%)
  local copies, waits for them, and re-layouts  9.89 us (22%)
  between operations  0.66 us (1%)
    pallas_call x1, Pallas kernels, on_device(): pl.pallas_call(functools.partial(kernel, n, count), out_shape=(jax.ShapeD...  33.5 us
    unnamed x19, local copies, waits for them, and re-layouts  9.89 us

profile of v1, /device:TPU:14, one launch (start us, length us, event | category | flops | bytes accessed | tf_op | source)
XLA Modules:
  0.0 44.1 jit_solution(13892831503981680371)
XLA Ops:
  0.6 0.0 copy-start
  0.6 1.4 %copy-done = f32[6,2,256,128]{3,2,1,0:T(8,128)S(1)} copy-done((f32[6,2,256,128]{3,2,1,0:T(8,128)S(1)}, f32[6,2,256,128]{3,2,1,0:T(8,128)}, u32[]{:S(2)}) %copy-start) | copy-done | bytes 1572888
  2.0 0.0 copy-start.1
  2.0 0.9 %copy-done.1 = s32[2,256,128]{2,1,0:T(8,128)S(1)} copy-done((s32[2,256,128]{2,1,0:T(8,128)S(1)}, s32[2,256,128]{2,1,0:T(8,128)}, u32[]{:S(2)}) %copy-start.1) | copy-done | bytes 262168
  3.0 0.0 copy-start.2
  3.0 0.9 %copy-done.2 = f32[2,128,256]{2,1,0:T(8,128)S(1)} copy-done((f32[2,128,256]{2,1,0:T(8,128)S(1)}, f32[2,128,256]{2,1,0:T(8,128)}, u32[]{:S(2)}) %copy-start.2) | copy-done | bytes 262168
  3.9 0.0 copy-start.3
  3.9 0.9 %copy-done.3 = f32[2,128,256]{2,1,0:T(8,128)S(1)} copy-done((f32[2,128,256]{2,1,0:T(8,128)S(1)}, f32[2,128,256]{2,1,0:T(8,128)}, u32[]{:S(2)}) %copy-start.3) | copy-done | bytes 262168
  4.9 0.0 copy-start.4
  4.9 0.9 %copy-done.4 = s32[2,128,256]{2,1,0:T(8,128)S(1)} copy-done((s32[2,128,256]{2,1,0:T(8,128)S(1)}, s32[2,128,256]{2,1,0:T(8,128)}, u32[]{:S(2)}) %copy-start.4) | copy-done | bytes 262168
  5.8 0.0 copy-start.5
  5.8 0.7 %copy-done.5 = f32[8]{0:T(128)S(1)} copy-done((f32[8]{0:T(128)S(1)}, f32[8]{0:T(128)}, u32[]{:S(2)}) %copy-start.5) | copy-done | bytes 56
  6.5 0.0 copy-start.6
  6.5 0.7 %copy-done.6 = f32[8]{0:T(128)S(1)} copy-done((f32[8]{0:T(128)S(1)}, f32[8]{0:T(128)}, u32[]{:S(2)}) %copy-start.6) | copy-done | bytes 56
  7.2 0.0 copy-start.7
  7.2 0.7 %copy-done.7 = f32[16]{0:T(128)S(1)} copy-done((f32[16]{0:T(128)S(1)}, f32[16]{0:T(128)}, u32[]{:S(2)}) %copy-start.7) | copy-done | bytes 88
  7.8 33.5 %shard_map.112 = (f32[2,128,256]{2,1,0:T(8,128)S(1)}, f32[6,2,256,128]{3,2,1,0:T(8,128)S(1)}, f32[3,2,256,128]{3,2,1,0:T(8,128)S(1)}) custom-call(f32[6,2,256,128]{3,2,1,0:T(8,128)S(1)} %copy-done, f32[6,2,256,128]{3,2,1,0:T(8,128)} %s_hbm.1, s32[2,256,128]{2,1,0:T(8,128)S(1)} %copy-done.1, f32[8]{0:T(128)S(1)} %copy-done.5, f32[8]{0:T(128)S(1)} %copy-done.6, ...), custom_call_target="tpu_custom_call" | custom-call | tf_op jit(solution)/shard_map/pallas_call | solution.py:555
  41.3 0.7 %copy.15 = f32[2,128,256]{2,1,0:T(8,128)} copy(f32[2,128,256]{2,1,0:T(8,128)S(1)} %get-tuple-element.6) | data formatting | bytes 524288
  42.0 1.1 %copy.16 = f32[6,2,256,128]{3,2,1,0:T(8,128)} copy(f32[6,2,256,128]{3,2,1,0:T(8,128)S(1)} %get-tuple-element.7) | data formatting | bytes 3145728
  43.2 0.9 %copy.17 = f32[3,2,256,128]{3,2,1,0:T(8,128)} copy(f32[3,2,256,128]{3,2,1,0:T(8,128)S(1)} %get-tuple-element.8) | data formatting | bytes 1572864
Async XLA Ops:
  0.6 1.4 %copy-start = (f32[6,2,256,128]{3,2,1,0:T(8,128)S(1)}, f32[6,2,256,128]{3,2,1,0:T(8,128)}, u32[]{:S(2)}) copy-start(f32[6,2,256,128]{3,2,1,0:T(8,128)} %e_hbm.1) | copy-start | bytes 4718596
  2.0 0.9 %copy-start.1 = (s32[2,256,128]{2,1,0:T(8,128)S(1)}, s32[2,256,128]{2,1,0:T(8,128)}, u32[]{:S(2)}) copy-start(s32[2,256,128]{2,1,0:T(8,128)} %m_hbm.1) | copy-start | bytes 786436
  3.0 0.9 %copy-start.2 = (f32[2,128,256]{2,1,0:T(8,128)S(1)}, f32[2,128,256]{2,1,0:T(8,128)}, u32[]{:S(2)}) copy-start(f32[2,128,256]{2,1,0:T(8,128)} %p_hbm.1) | copy-start | bytes 786436
  3.9 0.9 %copy-start.3 = (f32[2,128,256]{2,1,0:T(8,128)S(1)}, f32[2,128,256]{2,1,0:T(8,128)}, u32[]{:S(2)}) copy-start(f32[2,128,256]{2,1,0:T(8,128)} %st_hbm.1) | copy-start | bytes 786436
  4.9 0.9 %copy-start.4 = (s32[2,128,256]{2,1,0:T(8,128)S(1)}, s32[2,128,256]{2,1,0:T(8,128)}, u32[]{:S(2)}) copy-start(s32[2,128,256]{2,1,0:T(8,128)} %c_hbm.1) | copy-start | bytes 786436
  5.8 0.7 %copy-start.5 = (f32[8]{0:T(128)S(1)}, f32[8]{0:T(128)}, u32[]{:S(2)}) copy-start(f32[8]{0:T(128)} %coh.1) | copy-start | bytes 100
  6.5 0.7 %copy-start.6 = (f32[8]{0:T(128)S(1)}, f32[8]{0:T(128)}, u32[]{:S(2)}) copy-start(f32[8]{0:T(128)} %fri.1) | copy-start | bytes 100
  7.2 0.7 %copy-start.7 = (f32[16]{0:T(128)S(1)}, f32[16]{0:T(128)}, u32[]{:S(2)}) copy-start(f32[16]{0:T(128)} %ptab.1) | copy-start | bytes 196

commit v2 on v1

--- a/solution.py
+++ b/solution.py
@@ -56,6 +56,8 @@
     CX,
     PN,
     EP,
+    ET,
+    ETR,
     PM,
     EM,
     T,
@@ -64,6 +66,8 @@
     SLR,
     RM,
     RMR,
+    RT,
+    RTR,
     OUTP,
     loc,
     snd,
@@ -115,7 +119,7 @@
         HX[0] = jnp.zeros(HX.shape[1:], F32)
         HF[0] = jnp.zeros(HF.shape[1:], F32)
         PM[0] = jnp.zeros(PM.shape[1:], F32)
-        EM[0] = jnp.zeros(EM.shape[1:], F32)
+        ETR[0] = jnp.zeros(ETR.shape[1:], F32)
         SLR[...] = jnp.zeros(SLR.shape, F32)
 
     @pl.when(jnp.logical_not(has_hi))
@@ -125,11 +129,11 @@
 
     @pl.when(h == 0)
     def _():
-        EM[...] = jnp.zeros(EM.shape, F32)
-        RMR[...] = jnp.zeros(RMR.shape, F32)
+        ETR[...] = jnp.zeros(ETR.shape, F32)
+        RTR[...] = jnp.zeros(RTR.shape, F32)
 
     PM[:, 0:PAD, :] = jnp.zeros((3, PAD, LANES), F32)
-    EM[:, 0:PAD, :] = jnp.zeros((2, PAD, LANES), F32)
+    EM[0:PAD, :] = jnp.zeros((PAD, LANES), F32)
     T[:, :, 0:PAD, :] = jnp.zeros((6, 2, PAD, LANES), F32)
 
     barrier = pltpu.get_barrier_semaphore()
@@ -188,7 +192,7 @@
     hi_f = remote(F1.at[chunks, 1, inner], HF.at[0], g + 1, h)
     lo_fy = remote(F1.at[:, :, pl.ds(PAD, PAD)], F1.at[:, :, pl.ds(PAD + ny, PAD)], g, h - 1)
     hi_fy = remote(F1.at[:, :, pl.ds(ny, PAD)], F1.at[:, :, pl.ds(0, PAD)], g, h + 1)
-    rim = remote(RM, RMR, g, h + 1)
+    rim = remote(RT, RTR, g, h + 1)
     slab = remote(SL, SLR, g + 1, h)
 
     def begin(lo, hi, at, size):
@@ -305,6 +309,10 @@
 
     lax.fori_loop(0, ym // ROWS, force_step, 0)
 
+    for b in range(ym // LANES):
+        block = slice(b * LANES, (b + 1) * LANES)
+        RT[:, block] = jnp.transpose(RM[block, :])[0:16]
+
     @pl.when(h < n - 1)
     def _():
         rim.start()
@@ -372,6 +380,12 @@
     def _():
         rim.wait_recv()
 
+    for b in range(ym // LANES):
+        block = slice(b * LANES, (b + 1) * LANES)
+        RMR[block, :] = jnp.transpose(
+            jnp.concatenate([RTR[:, block], jnp.zeros((LANES - 16, LANES), F32)], axis=0)
+        )
+
     def slab_step(i, _):
         rows = pl.ds(pl.multiple_of(i * ROWS, ROWS), ROWS)
         got = RMR[rows, :]
@@ -380,10 +394,6 @@
         return 0
 
     lax.fori_loop(0, ym // ROWS, slab_step, 0)
-
-    @pl.when(has_hi)
-    def _():
-        slab.start()
 
     arrive(lo_f, hi_f, g, count)
     arrive(lo_fy, hi_fy, h, n)
@@ -421,13 +431,19 @@
 
     lax.fori_loop(0, ny // ROWS, sweep_two, 0)
 
+    for c in range(1, n):
+        cols = EP[c]
+        if ny < LANES:
+            cols = jnp.concatenate([cols, jnp.zeros((LANES - ny, LANES), F32)], axis=0)
+        ET[c] = jnp.transpose(cols)[0:PAD]
+
     mine, ahead = [], []
     for d in range(1, n):
         to = lax.rem(h + d, n)
-        mine.append((to, remote(PN.at[to], PM.at[pl.ds(1, 2), prow_of(h)], g, to), remote(EP.at[to], EM.at[1, prow_of(h)], g, to)))
+        mine.append((to, remote(PN.at[to], PM.at[pl.ds(1, 2), prow_of(h)], g, to), remote(ET.at[to], ETR.at[1, h], g, to)))
     for d in range(n):
         to = lax.rem(h + d, n)
-        ahead.append((to, remote(PN.at[to, 1], PM.at[0, prow_of(h)], g + 1, to), remote(EP.at[to], EM.at[0, prow_of(h)], g + 1, to)))
+        ahead.append((to, remote(PN.at[to, 1], PM.at[0, prow_of(h)], g + 1, to), remote(ET.at[to], ETR.at[0, h], g + 1, to)))
     for to, body, brim in mine:
         body.start()
 
@@ -444,13 +460,17 @@
             def _():
                 brim.start()
 
+    @pl.when(has_hi)
+    def _():
+        slab.start()
+
     pn_out = local(OUTP, pn_hbm)
     pn_out.start()
     PM[1:3, prow_of(h), :] = PN[h]
 
     @pl.when(h > 0)
     def _():
-        EM[1, prow_of(h), :] = EP[h]
+        ETR[1, h] = ET[h]
 
     @pl.when(has_lo)
     def _():
@@ -471,6 +491,12 @@
             @pl.when(h > 0)
             def _():
                 brim.wait_recv()
+
+    for c in range(n):
+        parts = [ETR[0, c], ETR[1, c], jnp.zeros((LANES - 2 * PAD, LANES), F32)]
+        EM[PAD + c * ny : PAD + (c + 1) * ny, :] = jnp.transpose(
+            jnp.concatenate(parts, axis=0)
+        )[0:ny]
 
     def last_step(i, _):
         rows = pl.ds(pl.multiple_of(i * ROWS, ROWS), ROWS)
@@ -482,12 +508,7 @@
             parts = []
             for at in (prow, urow):
                 p = PM[j, at, :]
-                if j == 0:
-                    edge = pltpu.roll(EM[0, at, :], LANES - 1, 1)
-                elif j == 1:
-                    edge = EM[1, at, :]
-                else:
-                    edge = pltpu.roll(EM[1, at, :], LANES - 1, 1)
+                edge = pltpu.roll(EM[at, :], LANES - (1, PAD, PAD + 1)[j], 1)
                 pz = jnp.where(first, edge, pltpu.roll(p, 1, 1))
                 parts.append((p + pz, pz - p))
             (s0, d0), (s1, d1) = parts
@@ -545,7 +566,7 @@
     strain_inc, pressure = args[0], args[5]
     planes, ym = strain_inc.shape[1], strain_inc.shape[2]
     ny = pressure.shape[1]
-    assert planes == 2 and strain_inc.shape[3] == LANES and pressure.shape[2] == n * LANES
+    assert ny <= LANES and ym % LANES == 0 and planes == 2 and strain_inc.shape[3] == LANES and pressure.shape[2] == n * LANES
     vm = lambda *shape: pltpu.VMEM(shape, F32)
     vi = lambda *shape: pltpu.VMEM(shape, jnp.int32)
     any_spec = pl.BlockSpec(memory_space=pl.ANY)
@@ -577,21 +598,25 @@
             vm(3, n, ny, LANES),
             vm(n, 2, ny, LANES),
             vm(n, ny, LANES),
+            vm(n, PAD, LANES),
+            vm(2, n, PAD, LANES),
             vm(3, PAD + ym, LANES),
-            vm(2, PAD + ym, LANES),
+            vm(PAD + ym, LANES),
             vm(6, 2, PAD + ym, LANES),
             vm(3, 2, ym, LANES),
             vm(3, ym, LANES),
             vm(3, ym, LANES),
             vm(ym, LANES),
             vm(ym, LANES),
+            vm(16, ym),
+            vm(16, ym),
             vm(2, ny, n * LANES),
             pltpu.SemaphoreType.DMA((loads,)),
             pltpu.SemaphoreType.DMA((sends,)),
             pltpu.SemaphoreType.DMA((sends,)),
         ],
         compiler_params=pltpu.CompilerParams(
-            collective_id=0, has_side_effects=True, vmem_limit_bytes=48 * 1024 * 1024
+            collective_id=0, has_side_effects=True, vmem_limit_bytes=63 * 1024 * 1024
         ),
     )(*args)
 

time: 44.4 us -> 38.2 us (0.86)
  the two profiles are of different devices: /device:TPU:14 before, /device:TPU:8 now
where the time goes in v2:
time: 38.2 us; the launch traced here: 38 us
  Pallas kernels  32.1 us (84%)
  local copies, waits for them, and re-layouts  5.28 us (14%)
  between operations  0.64 us (2%)
    pallas_call x1, Pallas kernels, on_device(): pl.pallas_call(functools.partial(kernel, n, count), out_shape=(jax.ShapeD...  32.1 us
    unnamed x5, local copies, waits for them, and re-layouts  5.28 us

profile of v2, /device:TPU:8, one launch (start us, length us, event | category | flops | bytes accessed | tf_op | source)
XLA Modules:
  0.0 38.0 jit_solution(14119481282058314938)
XLA Ops:
  0.6 32.1 %shard_map.112 = (f32[2,128,256]{2,1,0:T(8,128)}, f32[6,2,256,128]{3,2,1,0:T(8,128)}, f32[3,2,256,128]{3,2,1,0:T(8,128)}) custom-call(f32[6,2,256,128]{3,2,1,0:T(8,128)} %e_hbm.1, f32[6,2,256,128]{3,2,1,0:T(8,128)} %s_hbm.1, s32[2,256,128]{2,1,0:T(8,128)} %m_hbm.1, f32[8]{0:T(128)} %coh.1, f32[8]{0:T(128)} %fri.1, f32[2,128,256]{2,1,0:T(8,128)} %p_hbm.1, ...), custom_call_target="tpu_custom_call" | custom-call | tf_op jit(solution)/shard_map/pallas_call | solution.py:576
  32.7 1.7 %copy.15 = f32[2,128,256]{2,1,0:T(8,128)} copy(f32[2,128,256]{2,1,0:T(8,128)} %get-tuple-element.6) | data formatting | bytes 524288
  34.4 0.0 copy-start
  34.4 2.7 %copy.16 = f32[6,2,256,128]{3,2,1,0:T(8,128)} copy(f32[6,2,256,128]{3,2,1,0:T(8,128)} %get-tuple-element.7) | data formatting | bytes 3145728
  37.1 0.0 copy-done
  37.1 0.9 %copy.17 = f32[3,2,256,128]{3,2,1,0:T(8,128)} copy(f32[3,2,256,128]{3,2,1,0:T(8,128)S(1)} %copy-done) | data formatting | bytes 1572864
Async XLA Ops:
  34.4 2.7 %copy-start = (f32[3,2,256,128]{3,2,1,0:T(8,128)S(1)}, f32[3,2,256,128]{3,2,1,0:T(8,128)}, u32[]{:S(2)}) copy-start(f32[3,2,256,128]{3,2,1,0:T(8,128)} %get-tuple-element.8) | copy-start | bytes 2359300

commit v3 on v2

--- a/solution.py
+++ b/solution.py
@@ -157,7 +157,7 @@
         SR[:, rows, :] = E[0, :, rows, :] + E[1, :, rows, :] + E[2, :, rows, :]
         return 0
 
-    lax.fori_loop(0, ym // 16, rate_step, 0)
+    lax.fori_loop(0, ym // 16, rate_step, 0, unroll=4)
     for cp in ld_c:
         cp.wait()
     ptable = [ptab[j] for j in range(ptab.shape[0])]
@@ -170,7 +170,7 @@
             )[0][0]
         return 0
 
-    lax.fori_loop(0, ny // ROWS, cond_step, 0)
+    lax.fori_loop(0, ny // ROWS, cond_step, 0, unroll=4)
     for cp in ld_p:
         cp.wait()
 
@@ -256,7 +256,7 @@
             T[c, :, prow, :] = out + mean if c < 3 else out
         return 0
 
-    lax.fori_loop(0, ym // ROWS, plastic_step, 0)
+    lax.fori_loop(0, ym // ROWS, plastic_step, 0, unroll=4)
     st_out = local(T.at[:, :, pl.ds(PAD, ym)], so_hbm)
     st_out.start()
 
@@ -307,7 +307,7 @@
         RM[rows, :] = packed
         return 0
 
-    lax.fori_loop(0, ym // ROWS, force_step, 0)
+    lax.fori_loop(0, ym // ROWS, force_step, 0, unroll=4)
 
     for b in range(ym // LANES):
         block = slice(b * LANES, (b + 1) * LANES)
@@ -372,7 +372,7 @@
                 F1[c, a, prow, :] = num * inverse
         return 0
 
-    lax.fori_loop(0, ny // ROWS, sweep_one, 0)
+    lax.fori_loop(0, ny // ROWS, sweep_one, 0, unroll=4)
     begin(lo_f, hi_f, g, count)
     begin(lo_fy, hi_fy, h, n)
 
@@ -393,7 +393,7 @@
             SL[r, rows, :] = SL[r, rows, :] + jnp.where(first, pltpu.roll(got, LANES - 6 - r, 1), 0.0)
         return 0
 
-    lax.fori_loop(0, ym // ROWS, slab_step, 0)
+    lax.fori_loop(0, ym // ROWS, slab_step, 0, unroll=4)
 
     arrive(lo_f, hi_f, g, count)
     arrive(lo_fy, hi_fy, h, n)
@@ -429,7 +429,7 @@
             EP[c, rows, :] = jnp.where(first, left, right)
         return 0
 
-    lax.fori_loop(0, ny // ROWS, sweep_two, 0)
+    lax.fori_loop(0, ny // ROWS, sweep_two, 0, unroll=4)
 
     for c in range(1, n):
         cols = EP[c]
@@ -525,7 +525,7 @@
                 FS[r, j, rows, :] = total
         return 0
 
-    lax.fori_loop(0, ym // ROWS, last_step, 0)
+    lax.fori_loop(0, ym // ROWS, last_step, 0, unroll=4)
     f_out = local(FS, f_hbm)
     f_out.start()
 
@@ -576,9 +576,9 @@
     return pl.pallas_call(
         functools.partial(kernel, n, count),
         out_shape=(
-            jax.ShapeDtypeStruct(pressure.shape, F32),
-            jax.ShapeDtypeStruct(strain_inc.shape, F32),
-            jax.ShapeDtypeStruct((3,) + strain_inc.shape[1:], F32),
+            pltpu.VMEM(pressure.shape, F32),
+            pltpu.VMEM(strain_inc.shape, F32),
+            pltpu.VMEM((3,) + strain_inc.shape[1:], F32),
         ),
         in_specs=[any_spec, any_spec, any_spec, smem, smem, any_spec, any_spec, any_spec, smem],
         out_specs=(any_spec, any_spec, any_spec),
@@ -616,7 +616,7 @@
             pltpu.SemaphoreType.DMA((sends,)),
         ],
         compiler_params=pltpu.CompilerParams(
-            collective_id=0, has_side_effects=True, vmem_limit_bytes=63 * 1024 * 1024
+            collective_id=0, has_side_effects=True, vmem_limit_bytes=56 * 1024 * 1024
         ),
     )(*args)
 

time: 38.2 us -> 28.6 us (0.75)
  the two profiles are of different devices: /device:TPU:8 before, /device:TPU:4 now
where the time goes in v3:
time: 28.6 us; the launch traced here: 28.4 us
  Pallas kernels  25 us (87%)
  local copies, waits for them, and re-layouts  2.73 us (10%)
  between operations  0.64 us (2%)
    pallas_call x1, Pallas kernels, on_device(): pl.pallas_call(functools.partial(kernel, n, count), out_shape=(pltpu.VMEM...  25 us
    unnamed x3, local copies, waits for them, and re-layouts  2.73 us

profile of v3, /device:TPU:4, one launch (start us, length us, event | category | flops | bytes accessed | tf_op | source)
XLA Modules:
  0.0 28.4 jit_solution(16526170359925149748)
XLA Ops:
  0.6 25.0 %shard_map.112 = (f32[2,128,256]{2,1,0:T(8,128)S(1)}, f32[6,2,256,128]{3,2,1,0:T(8,128)S(1)}, f32[3,2,256,128]{3,2,1,0:T(8,128)S(1)}) custom-call(f32[6,2,256,128]{3,2,1,0:T(8,128)} %e_hbm.1, f32[6,2,256,128]{3,2,1,0:T(8,128)} %s_hbm.1, s32[2,256,128]{2,1,0:T(8,128)} %m_hbm.1, f32[8]{0:T(128)} %coh.1, f32[8]{0:T(128)} %fri.1, f32[2,128,256]{2,1,0:T(8,128)} %p_hbm.1, ...), custom_call_target="tpu_custom_call" | custom-call | tf_op jit(solution)/shard_map/pallas_call | solution.py:576
  25.7 0.7 %copy.15 = f32[2,128,256]{2,1,0:T(8,128)} copy(f32[2,128,256]{2,1,0:T(8,128)S(1)} %get-tuple-element.3) | data formatting | bytes 524288
  26.4 0.9 %copy.17 = f32[3,2,256,128]{3,2,1,0:T(8,128)} copy(f32[3,2,256,128]{3,2,1,0:T(8,128)S(1)} %get-tuple-element.5) | data formatting | bytes 1572864
  27.3 1.1 %copy.16 = f32[6,2,256,128]{3,2,1,0:T(8,128)} copy(f32[6,2,256,128]{3,2,1,0:T(8,128)S(1)} %get-tuple-element.4) | data formatting | bytes 3145728

commit v4 on v3

--- a/solution.py
+++ b/solution.py
@@ -157,7 +157,7 @@
         SR[:, rows, :] = E[0, :, rows, :] + E[1, :, rows, :] + E[2, :, rows, :]
         return 0
 
-    lax.fori_loop(0, ym // 16, rate_step, 0, unroll=4)
+    lax.fori_loop(0, ym // 16, rate_step, 0, unroll=8)
     for cp in ld_c:
         cp.wait()
     ptable = [ptab[j] for j in range(ptab.shape[0])]
@@ -170,7 +170,7 @@
             )[0][0]
         return 0
 
-    lax.fori_loop(0, ny // ROWS, cond_step, 0, unroll=4)
+    lax.fori_loop(0, ny // ROWS, cond_step, 0, unroll=min(8, ny // ROWS))
     for cp in ld_p:
         cp.wait()
 
@@ -256,7 +256,7 @@
             T[c, :, prow, :] = out + mean if c < 3 else out
         return 0
 
-    lax.fori_loop(0, ym // ROWS, plastic_step, 0, unroll=4)
+    lax.fori_loop(0, ym // ROWS, plastic_step, 0, unroll=8)
     st_out = local(T.at[:, :, pl.ds(PAD, ym)], so_hbm)
     st_out.start()
 
@@ -307,7 +307,7 @@
         RM[rows, :] = packed
         return 0
 
-    lax.fori_loop(0, ym // ROWS, force_step, 0, unroll=4)
+    lax.fori_loop(0, ym // ROWS, force_step, 0, unroll=8)
 
     for b in range(ym // LANES):
         block = slice(b * LANES, (b + 1) * LANES)
@@ -372,7 +372,7 @@
                 F1[c, a, prow, :] = num * inverse
         return 0
 
-    lax.fori_loop(0, ny // ROWS, sweep_one, 0, unroll=4)
+    lax.fori_loop(0, ny // ROWS, sweep_one, 0, unroll=min(8, ny // ROWS))
     begin(lo_f, hi_f, g, count)
     begin(lo_fy, hi_fy, h, n)
 
@@ -393,7 +393,7 @@
             SL[r, rows, :] = SL[r, rows, :] + jnp.where(first, pltpu.roll(got, LANES - 6 - r, 1), 0.0)
         return 0
 
-    lax.fori_loop(0, ym // ROWS, slab_step, 0, unroll=4)
+    lax.fori_loop(0, ym // ROWS, slab_step, 0, unroll=8)
 
     arrive(lo_f, hi_f, g, count)
     arrive(lo_fy, hi_fy, h, n)
@@ -429,7 +429,7 @@
             EP[c, rows, :] = jnp.where(first, left, right)
         return 0
 
-    lax.fori_loop(0, ny // ROWS, sweep_two, 0, unroll=4)
+    lax.fori_loop(0, ny // ROWS, sweep_two, 0, unroll=min(8, ny // ROWS))
 
     for c in range(1, n):
         cols = EP[c]
@@ -525,7 +525,7 @@
                 FS[r, j, rows, :] = total
         return 0
 
-    lax.fori_loop(0, ym // ROWS, last_step, 0, unroll=4)
+    lax.fori_loop(0, ym // ROWS, last_step, 0, unroll=8)
     f_out = local(FS, f_hbm)
     f_out.start()
 

time: 28.6 us -> 27.8 us (0.972)
  Pallas kernels: 25 us -> 24.3 us
    pallas_call x1, Pallas kernels: 25 us -> 24.3 us  [on_device(): pl.pallas_call(functools.partial(kernel, n, count), out_shape=(pltpu.VMEM...]
where the time goes in v4:
time: 27.8 us; the launch traced here: 27.7 us
  Pallas kernels  24.3 us (87%)
  local copies, waits for them, and re-layouts  2.73 us (10%)
  between operations  0.64 us (2%)
    pallas_call x1, Pallas kernels, on_device(): pl.pallas_call(functools.partial(kernel, n, count), out_shape=(pltpu.VMEM...  24.3 us
    unnamed x3, local copies, waits for them, and re-layouts  2.73 us

profile of v4, /device:TPU:4, one launch (start us, length us, event | category | flops | bytes accessed | tf_op | source)
XLA Modules:
  0.0 27.7 jit_solution(17231290893288297249)
XLA Ops:
  0.6 24.3 %shard_map.112 = (f32[2,128,256]{2,1,0:T(8,128)S(1)}, f32[6,2,256,128]{3,2,1,0:T(8,128)S(1)}, f32[3,2,256,128]{3,2,1,0:T(8,128)S(1)}) custom-call(f32[6,2,256,128]{3,2,1,0:T(8,128)} %e_hbm.1, f32[6,2,256,128]{3,2,1,0:T(8,128)} %s_hbm.1, s32[2,256,128]{2,1,0:T(8,128)} %m_hbm.1, f32[8]{0:T(128)} %coh.1, f32[8]{0:T(128)} %fri.1, f32[2,128,256]{2,1,0:T(8,128)} %p_hbm.1, ...), custom_call_target="tpu_custom_call" | custom-call | tf_op jit(solution)/shard_map/pallas_call | solution.py:576
  25.0 0.7 %copy.15 = f32[2,128,256]{2,1,0:T(8,128)} copy(f32[2,128,256]{2,1,0:T(8,128)S(1)} %get-tuple-element.3) | data formatting | bytes 524288
  25.7 0.9 %copy.17 = f32[3,2,256,128]{3,2,1,0:T(8,128)} copy(f32[3,2,256,128]{3,2,1,0:T(8,128)S(1)} %get-tuple-element.5) | data formatting | bytes 1572864
  26.5 1.1 %copy.16 = f32[6,2,256,128]{3,2,1,0:T(8,128)} copy(f32[6,2,256,128]{3,2,1,0:T(8,128)S(1)} %get-tuple-element.4) | data formatting | bytes 3145728
